TPU v7x, 32 devices: a whole 2x2x4 slice. The times are simulated.
32 devices in a mesh: head: 2 (over x), ctx: 16 (over z, y, core).
Axes of the slice: x: 2, y: 2, z: 4, core: 2. Of those that a mesh axis runs over, the one named last changes fastest.
Arguments:
- query_bits: int32 [256, 4096], P('head', 'ctx'), may hold values from 0 to 65535
- key_bits: int32 [256, 4096], P('head', 'ctx'), may hold values from 0 to 65535
- values: bfloat16 [4096, 4096], P('ctx', 'head'), may hold values from -6 to 6
- grad_out: bfloat16 [16, 256, 4096], P('ctx', 'head'), may hold values from -6 to 6
- tile_mask: int32 [16, 2, 2], P('ctx'), may hold values 0 or 1
Outputs:
- query_grad: bfloat16 [4096, 4096], P('ctx', 'head')
- key_grad: bfloat16 [4096, 4096], P('ctx', 'head')
- value_grad: bfloat16 [4096, 4096], P('ctx', 'head')
All inputs are finite; a program needn't handle non-finite values. No bound on the sum of `tile_mask` on one device may be relied on, other than what follows from the above.
Results may differ from a plain program's by a relative error of at most 0.0049.
Values may be sent and summed in bfloat16 or wider, within the bound.
A program may use at most 128 MiB of HBM per device.

v0:
```python
import math

import jax
import jax.numpy as jnp
from jax import lax
from jax.sharding import PartitionSpec as P

HD = 128


def carried_in(part, axis, combine, identity, reverse):
    count = lax.axis_size(axis)
    place = lax.axis_index(axis)
    ahead = count - 1 - place if reverse else place
    gathered = lax.all_gather(part, axis)
    state = jnp.zeros_like(part) + jnp.asarray(identity, part.dtype)

    def one(step, state):
        source = count - 1 - step if reverse else step
        return combine(state, lax.dynamic_index_in_dim(gathered, source, 0, False))

    return lax.fori_loop(0, ahead, one, state)


def unpack_bits(packed, heads_here):
    shifts = jnp.arange(16, dtype=jnp.int32).reshape(1, 1, 16, 1)
    spread = jnp.right_shift(packed.reshape(heads_here, -1, 1, packed.shape[-1]), shifts)
    return jnp.bitwise_and(spread, 1).astype(jnp.bfloat16).reshape(heads_here, -1, packed.shape[-1])


def token_mask(tiles, tile_size):
    tile_count = tiles.shape[0]
    tile_index = jnp.arange(tile_count, dtype=jnp.int32)
    lower = tile_index[:, None] > tile_index[None, :]
    diagonal = tile_index[:, None] == tile_index[None, :]
    allowed = jnp.where(diagonal, 1.0, jnp.where(lower, tiles.astype(jnp.float32), 0.0))
    span_width = tile_count * tile_size
    expanded = jnp.broadcast_to(
        allowed[:, None, :, None], (tile_count, tile_size, tile_count, tile_size)
    ).reshape(span_width, span_width)
    position = jnp.arange(span_width, dtype=jnp.int32)
    return jnp.where(position[:, None] >= position[None, :], expanded, 0.0)


def stretch_grads(query_spk, key_spk, value_rows, grad_rows, state, adjoint, keep_mask, att_scale):
    pair_dots = jnp.dot(grad_rows, value_rows.T, preferred_element_type=jnp.float32)
    grad_weights = (att_scale * pair_dots * keep_mask).astype(jnp.bfloat16)
    spike_dots = jnp.dot(query_spk.T, key_spk, preferred_element_type=jnp.float32)
    att_weights = (att_scale * spike_dots * keep_mask).astype(jnp.bfloat16)
    query_grad = jnp.dot(
        grad_weights, key_spk.T, preferred_element_type=jnp.float32
    ) + att_scale * jnp.dot(grad_rows, state.T, preferred_element_type=jnp.float32)
    key_grad = jnp.dot(
        grad_weights.T, query_spk.T, preferred_element_type=jnp.float32
    ) + att_scale * jnp.dot(value_rows, adjoint.T, preferred_element_type=jnp.float32)
    value_grad = jnp.dot(
        att_weights.T, grad_rows, preferred_element_type=jnp.float32
    ) + att_scale * jnp.dot(key_spk.T, adjoint, preferred_element_type=jnp.float32)
    return (
        query_grad.astype(jnp.bfloat16),
        key_grad.astype(jnp.bfloat16),
        value_grad.astype(jnp.bfloat16),
    )


def add_terms(earlier, later):
    return earlier + later


def local(query_bits, key_bits, values, grad_out, tile_mask):
    tok_rows = values.shape[0]
    head_group = values.shape[1] // HD
    att_scale = 4.0 / (HD * math.sqrt(tok_rows * lax.axis_size("ctx")))
    query_spk = unpack_bits(query_bits, head_group)
    key_spk = unpack_bits(key_bits, head_group)
    value_heads = values.reshape(tok_rows, head_group, HD)
    state_term = jnp.einsum(
        "hdt,the->hde", key_spk, value_heads, preferred_element_type=jnp.float32
    )
    zero_state = jnp.zeros_like(state_term)
    state_sum = carried_in(state_term, "ctx", add_terms, zero_state, False)
    state = state_sum.astype(jnp.bfloat16)
    keep_mask = token_mask(tile_mask[0], tok_rows // tile_mask.shape[1])
    value_major = value_heads.transpose(1, 0, 2)

    def one_head(head_item):
        head_query, head_key, head_value, head_grad, head_state, head_adjoint = head_item
        return stretch_grads(
            head_query,
            head_key,
            head_value,
            head_grad,
            head_state,
            head_adjoint,
            keep_mask,
            att_scale,
        )

    grad_heads = lax.all_to_all(grad_out, "head", split_axis=2, concat_axis=1, tiled=True).reshape(
        tok_rows, head_group, HD
    )
    adjoint_term = jnp.einsum(
        "hdt,the->hde", query_spk, grad_heads, preferred_element_type=jnp.float32
    )
    adjoint_sum = carried_in(adjoint_term, "ctx", add_terms, zero_state, True)
    adjoint = adjoint_sum.astype(jnp.bfloat16)
    grads_query, grads_key, grads_value = lax.map(
        one_head, (query_spk, key_spk, value_major, grad_heads.transpose(1, 0, 2), state, adjoint)
    )
    return (
        grads_query.transpose(1, 0, 2).reshape(tok_rows, head_group * HD),
        grads_key.transpose(1, 0, 2).reshape(tok_rows, head_group * HD),
        grads_value.transpose(1, 0, 2).reshape(tok_rows, head_group * HD),
    )


def solution(mesh):
    return jax.shard_map(
        local,
        mesh=mesh,
        in_specs=(
            P("head", "ctx"),
            P("head", "ctx"),
            P("ctx", "head"),
            P("ctx", "head", None),
            P("ctx", None, None),
        ),
        out_specs=(P("ctx", "head"), P("ctx", "head"), P("ctx", "head")),
        check_vma=False,
    )
```

profile of v0, /device:TPU:1, one launch (start us, length us, event | category | flops | bytes accessed | tf_op | source)
XLA Modules:
  0.0 426.8 jit_solution(14961386463483998886)
XLA Ops:
  12.0 5.0 %copy.30 = bf16[1,128,4096]{1,0,2:T(2,128)(2,1)S(1)} copy(bf16[1,128,4096]{2,1,0:T(8,128)(2,1)} %param.14) | data formatting | bytes 2097152 | tf_op args[3]
  17.5 23.4 %reduce = bf16[4096,128]{1,0:T(8,128)(2,1)} reduce(bf16[4096,1,128]{2,1,0:T(2,128)(2,1)S(1)} %bitcast.167, bf16[]{:T(256)} %broadcast.52), dimensions={1}, to_apply=%bitcast.103.reduce_sub_computation | reduce | bytes 2097154
  42.3 17.1 %all_to_all.15 = bf16[2,2,131072]{2,1,0:T(2,128)(2,1)} all-to-all(bf16[2,2,131072]{2,1,0:T(2,128)(2,1)S(1)} %reshape.81), channel_id=1, replica_groups=mesh['head'=2,'ctx'=16] {'head'}, dimensions={0} | all-to-all | bytes 2097152 | tf_op jit(solution)/shard_map/all_to_all | solution.py:99
  59.4 2.0 reshape.82
  62.5 2.4 copy.31
  69.1 72.3 %all-gather.5.cloned.1.call-done = f32[256,128,128]{2,1,0:T(8,128)} async-done(((f32[16,128,128]{2,1,0:T(8,128)}), f32[256,128,128]{2,1,0:T(8,128)}) %all-gather.5.cloned.1.call-update) | async-done | bytes 16777232 | tf_op jit(solution)/shard_map/all_gather | solution.py:15
  144.0 124.7 %all-gather.7.cloned.1.call-done = f32[256,128,128]{2,1,0:T(8,128)} async-done(((f32[16,128,128]{2,1,0:T(8,128)}), f32[256,128,128]{2,1,0:T(8,128)}) %all-gather.7.cloned.1.call-update) | async-done | bytes 16777232 | tf_op jit(solution)/shard_map/all_gather | solution.py:15
  268.8 21.2 %while.38 = (s32[]{:T(128)}, f32[16,128,128]{2,1,0:T(8,128)S(1)}, s32[]{:T(128)}, f32[16,16,128,128]{3,2,1,0:T(8,128)}, s32[]{:T(128)}, /*index=5*/s32[]{:T(128)}, s32[]{:T(128)}, s32[]{:T(128)}) while((s32[]{:T(128)}, f32[16,128,128]{2,1,0:T(8,128)S(1)}, s32[]{:T(128)}, f32[16,16,128,128]{3,2,1,0:T(8,128)}, s32[]{:T(128)}, ...), condition=%wide.region_3.4_spmd, body=%wide.region_2.3_spmd.sunk | while | flops 262150 | bytes 3145863 | solution.py:22
  291.0 124.9 %while.39 = (s32[]{:T(128)}, bf16[16,256,128]{2,1,0:T(8,128)(2,1)}, bf16[16,256,128]{2,1,0:T(8,128)(2,1)}, bf16[16,256,128]{2,1,0:T(8,128)(2,1)}, bf16[16,256,12...) while((s32[]{:T(128)}, bf16[16,256,128]{2,1,0:T(8,128)(2,1)}, ...), condition=%wide.region_5.6_spmd.clone, body=%wide.region_4.5_spmd.clone.sunk | while | flops 110002176 | bytes 2924677 | solution.py:107
  296.9 1.9 fusion.111
  304.7 1.9 fusion.111
  320.3 1.9 fusion.111
  328.1 1.9 fusion.111
  335.9 1.9 fusion.111
  343.7 1.9 fusion.111
  351.5 1.9 fusion.111
  359.3 1.9 fusion.111
  374.9 1.9 fusion.111
  382.7 1.9 fusion.111
  390.5 1.9 fusion.111
  398.3 1.9 fusion.111
  406.1 1.9 fusion.111
  413.9 1.9 fusion.111
  415.9 2.5 copy_bitcast_fusion.2
  (168 shorter events, 137.0 us)
Async XLA Ops:
  7.2 1.7 copy-start.5
  7.2 1.7 copy-start.4
  7.2 134.3 %all-gather.5.cloned.1.call-start = ((), (), s32[]{:S(2)}) async-start(), calls=%async_computation.1 | async-start | bytes 17825792 | tf_op jit(solution)/shard_map/all_gather | solution.py:15
  8.8 3.1 copy-start.1
  11.9 256.8 %all-gather.7.cloned.1.call-start = ((), (), s32[]{:S(2)}) async-start(), calls=%async_computation.2 | async-start | bytes 17825792 | tf_op jit(solution)/shard_map/all_gather | solution.py:15
  62.5 3.9 copy-start
  66.4 1.5 copy-start.6
  415.9 2.5 copy-start.2
  415.9 2.5 copy-start.3
Sparse Core Ops, SparseCore 0:
  12.0 129.3 all-gather.4
  143.6 125.0 all-gather.6
where the time goes:
time: 434 us; the launch traced here: 427 us
  waiting for transfers between devices  197 us (45%)
  matrix products  125 us (29%)
  other arithmetic  49.1 us (11%)
  local copies, waits for them, and re-layouts  23.1 us (5%)
  blocking collectives  17.1 us (4%)
  between operations  14.2 us (3%)
    all_gather x2, waiting for transfers between devices, carried_in(): gathered = lax.all_gather(part, axis)  197 us
    dot_general x16, matrix products, stretch_grads(): jnp.dot(att_weights.T, grad_rows, preferred_element_type=jnp.float32)  30.8 us
    unnamed x1, other arithmetic  23.4 us
    add x15, other arithmetic, add_terms(): return earlier + later  22.3 us
    all_to_all x1, blocking collectives, local(): lax.all_to_all(grad_out, 'head', split_axis=2, concat_axis=1, tiled=True)  17.1 us
    dot_general x16, matrix products, stretch_grads(): jnp.dot(grad_rows, value_rows.T, preferred_element_type=jnp.float32)  16.8 us
    dot_general x16, matrix products, stretch_grads(): jnp.dot(value_rows, adjoint.T, preferred_element_type=jnp.float32)  16.5 us
    dot_general x16, matrix products, stretch_grads(): jnp.dot(grad_rows, state.T, preferred_element_type=jnp.float32)  16.1 us
  transfers between devices with their start and end apart: 2, of which 2 were waited for; matrix products, arithmetic and copies ran while one was open for 10% of the time, Pallas kernels for 0%

commit v1 on v0

v1 whole, which is shorter than its diff:
```python
import functools
import math

import jax
import jax.numpy as jnp
from jax import lax
from jax.experimental import pallas as pl
from jax.experimental.pallas import tpu as pltpu
from jax.sharding import PartitionSpec as P

HD = 128
CHUNK = 4
HALF = CHUNK // 2
MESH = pl.DeviceIdType.MESH
CORE, ROW, CHAIN, BACK = range(4)


def spikes(words_ref, head, words):
    bits = HD // words
    packed = words_ref[head * words : (head + 1) * words, :]
    shifts = lax.broadcasted_iota(jnp.int32, (words, bits, packed.shape[1]), 1)
    spread = jnp.right_shift(packed[:, None, :], shifts) & 1
    return spread.reshape(HD, packed.shape[1]).astype(jnp.float32).astype(jnp.bfloat16)


def scan_kernel(
    groups, stretches,
    query_ref, key_ref, value_hbm, grad_hbm,
    carry_hbm, heads_hbm,
    value_buf, grad_buf, carry, own, chip, core_out, core_in, row_out, row_in,
    chain_out, chain_in, back_out,
    send_sem, recv_sem, swap_send, swap_recv, local_sem, out_sem,
):
    tokens, width = value_buf.shape
    head_count = width // HD
    words = query_ref.shape[0] // head_count
    chunks = head_count // CHUNK
    part = tokens // groups
    group = lax.axis_index("head")
    place = lax.axis_index("ctx")
    core, row, plane = place % 2, (place // 2) % 2, place // 4
    planes = stretches // 4
    mate = (group, place + 1 - 2 * core)
    across = (group, place + 2 - 4 * row)
    above, below = (group, place + 4), (group, place - 4)
    has_above, has_below = plane < planes - 1, plane > 0
    partners = [(lax.rem(group + k, groups), place) for k in range(1, groups)]

    barrier = pltpu.get_barrier_semaphore()
    for device in partners + [mate, across]:
        pl.semaphore_signal(barrier, inc=1, device_id=device, device_id_type=MESH)

    @pl.when(has_above)
    def _():
        pl.semaphore_signal(barrier, inc=1, device_id=above, device_id_type=MESH)

    @pl.when(has_below)
    def _():
        pl.semaphore_signal(barrier, inc=1, device_id=below, device_id_type=MESH)

    def cols(chunk):
        return pl.ds(chunk * CHUNK * HD, CHUNK * HD)

    def grad_cols(owner, chunk):
        return pl.ds(pl.multiple_of(owner * width + chunk * CHUNK * HD, HD), CHUNK * HD)

    my_rows = pl.ds(pl.multiple_of(group * part, part), part)
    value_in = [
        pltpu.make_async_copy(value_hbm.at[:, cols(j)], value_buf.at[:, cols(j)], local_sem.at[0, j])
        for j in range(chunks)
    ]
    grad_in = [
        pltpu.make_async_copy(
            grad_hbm.at[0, :, grad_cols(group, j)], grad_buf.at[my_rows, cols(j)], local_sem.at[1, j]
        )
        for j in range(chunks)
    ]
    for copy in value_in + grad_in:
        copy.start()

    pl.semaphore_wait(
        barrier, groups + 1 + has_above.astype(jnp.int32) + has_below.astype(jnp.int32)
    )

    swaps = [
        [
            pltpu.make_async_remote_copy(
                src_ref=grad_hbm.at[0, :, grad_cols(device[0], j)],
                dst_ref=grad_buf.at[my_rows, cols(j)],
                send_sem=swap_send.at[k, j],
                recv_sem=swap_recv.at[k, j],
                device_id=device,
                device_id_type=MESH,
            )
            for k, device in enumerate(partners)
        ]
        for j in range(chunks)
    ]
    for copies in swaps:
        for copy in copies:
            copy.start()

    def remote(kind, which, j, src, dst, device):
        return pltpu.make_async_remote_copy(
            src_ref=src,
            dst_ref=dst,
            send_sem=send_sem.at[kind, which, j],
            recv_sem=recv_sem.at[kind, which, j],
            device_id=device,
            device_id_type=MESH,
        )

    def mine(j):
        return pl.ds(j * CHUNK + HALF * core, HALF)

    def core_copy(which, j):
        return remote(CORE, which, j, core_out.at[which, j], core_in.at[which, j], mate)

    def row_copy(which, j):
        return remote(ROW, which, j, row_out.at[which, j], row_in.at[which, j], across)

    def chain_copy(which, j):
        device = below if which else above
        return remote(CHAIN, which, j, chain_out.at[which, j], chain_in.at[which, j], device)

    def back_copy(which, j):
        return remote(BACK, which, j, back_out.at[which, j], carry.at[which, mine(j)], mate)

    first_core = core == 0

    def terms(which, j):
        if which == 0:
            value_in[j].wait()
        else:
            grad_in[j].wait()
            for copy in swaps[j]:
                copy.wait_recv()
        dots = []
        for head in range(j * CHUNK, (j + 1) * CHUNK):
            rows = value_buf if which == 0 else grad_buf
            spike = spikes(key_ref if which == 0 else query_ref, head, words)
            dots.append(
                jnp.dot(
                    spike, rows[:, head * HD : (head + 1) * HD], preferred_element_type=jnp.float32
                )
            )
        for i in range(HALF):
            low, high = dots[i], dots[HALF + i]
            own[which, j, i] = jnp.where(first_core, low, high)
            core_out[which, j, i] = jnp.where(first_core, high, low)
        core_copy(which, j).start()

    def chip_sum(which, j):
        core_copy(which, j).wait_recv()
        total = own[which, j] + core_in[which, j]
        chip[which, j] = total
        row_out[which, j] = total.astype(jnp.bfloat16)
        row_copy(which, j).start()

    def chain(which, j):
        starts, goes_on = (has_above, has_below) if which else (has_below, has_above)
        row_copy(which, j).wait_recv()

        @pl.when(starts)
        def _():
            chain_copy(which, j).wait_recv()

        @pl.when(jnp.logical_not(starts))
        def _():
            chain_in[which, j] = jnp.zeros_like(chain_in[which, j])

        base = chain_in[which, j].astype(jnp.float32)
        other = row_in[which, j].astype(jnp.float32)

        @pl.when(goes_on)
        def _():
            chain_out[which, j] = (base + other + chip[which, j]).astype(jnp.bfloat16)
            chain_copy(which, j).start()

        base = base + jnp.where(row == (1 - which), other, 0.0)
        nearer = first_core if which == 0 else jnp.logical_not(first_core)
        more = base + jnp.where(nearer, own[which, j], core_in[which, j])
        back_out[which, j] = jnp.where(nearer, more, base).astype(jnp.bfloat16)
        back_copy(which, j).start()
        carry[which, mine(j)] = jnp.where(nearer, base, more).astype(jnp.bfloat16)

    def carry_out(which, j):
        heads = pl.ds(j * CHUNK, CHUNK)
        return pltpu.make_async_copy(
            carry.at[which, heads], carry_hbm.at[which, heads], out_sem.at[which, j]
        )

    def heads_out(j):
        return pltpu.make_async_copy(
            grad_buf.at[:, cols(j)], heads_hbm.at[:, cols(j)], out_sem.at[2, j]
        )

    def land(which, j):
        back_copy(which, j).wait_recv()
        carry_out(which, j).start()

    for j in range(chunks + 1):
        if j < chunks:
            terms(0, j)
        if j > 0:
            chip_sum(0, j - 1)
    for j in range(chunks + 1):
        if j < chunks:
            terms(1, j)
            heads_out(j).start()
            chain(0, j)
            chip_sum(1, j)
        if j > 0:
            chain(1, j - 1)
    for which in range(2):
        for j in range(chunks):
            land(which, j)

    for j in range(chunks):
        for copy in swaps[j]:
            copy.wait_send()
        heads_out(j).wait()
        for which in range(2):
            core_copy(which, j).wait_send()
            row_copy(which, j).wait_send()
            back_copy(which, j).wait_send()

            @pl.when(has_below if which else has_above)
            def _():
                chain_copy(which, j).wait_send()

            carry_out(which, j).wait()


def grads_kernel(
    att_scale,
    tiles_ref, query_ref, key_ref, value_ref, grad_ref, state_ref, adjoint_ref,
    query_out, key_out, value_out,
):
    tokens = value_ref.shape[0]
    words = query_ref.shape[0] // CHUNK
    tile_count = tiles_ref.shape[1]
    size = tokens // tile_count
    t = lax.broadcasted_iota(jnp.int32, (tokens, tokens), 0)
    s = lax.broadcasted_iota(jnp.int32, (tokens, tokens), 1)

    def masked(t, s):
        keep = jnp.where((t >= s) & (t // size == s // size), att_scale, 0.0)
        for a in range(tile_count):
            for b in range(a):
                allowed = tiles_ref[0, a, b].astype(jnp.float32) * att_scale
                keep = jnp.where((t // size == a) & (s // size == b), allowed, keep)
        return keep

    keep, keep_t = masked(t, s), masked(s, t)

    def dot(a, b, dims=((1,), (0,))):
        return lax.dot_general(a, b, (dims, ((), ())), preferred_element_type=jnp.float32)

    last = ((1,), (1,))
    for i in range(CHUNK):
        columns = slice(i * HD, (i + 1) * HD)
        query = spikes(query_ref, i, words)
        key_t = spikes(key_ref, i, words).T
        value = value_ref[:, columns]
        grad = grad_ref[:, columns]
        weights = (dot(grad, value, last) * keep).astype(jnp.bfloat16)
        weights_t = (dot(value, grad, last) * keep_t).astype(jnp.bfloat16)
        att_t = (dot(key_t, query) * keep_t).astype(jnp.bfloat16)
        query_out[:, columns] = (
            dot(weights, key_t) + att_scale * dot(grad, state_ref[0, i], last)
        ).astype(jnp.bfloat16)
        key_out[:, columns] = (
            dot(weights_t, query, last) + att_scale * dot(value, adjoint_ref[0, i], last)
        ).astype(jnp.bfloat16)
        value_out[:, columns] = (
            dot(att_t, grad) + att_scale * dot(key_t, adjoint_ref[0, i])
        ).astype(jnp.bfloat16)


def local(query_bits, key_bits, values, grad_out, tile_mask):
    groups, stretches = lax.axis_size("head"), lax.axis_size("ctx")
    tokens, width = values.shape
    heads = width // HD
    chunks = heads // CHUNK
    att_scale = 4.0 / (HD * math.sqrt(tokens * stretches))
    bf16, f32 = jnp.bfloat16, jnp.float32
    slots = (2, chunks, HALF, HD, HD)
    vmem, any_space = pl.BlockSpec(memory_space=pltpu.VMEM), pl.BlockSpec(memory_space=pl.ANY)
    carry, grad_heads = pl.pallas_call(
        functools.partial(scan_kernel, groups, stretches),
        out_shape=(
            jax.ShapeDtypeStruct((2, heads, HD, HD), bf16),
            jax.ShapeDtypeStruct((tokens, width), bf16),
        ),
        in_specs=[vmem, vmem, any_space, any_space],
        out_specs=(any_space, any_space),
        scratch_shapes=[
            pltpu.VMEM((tokens, width), bf16),
            pltpu.VMEM((tokens, width), bf16),
            pltpu.VMEM((2, heads, HD, HD), bf16),
            pltpu.VMEM(slots, f32),
            pltpu.VMEM(slots, f32),
            pltpu.VMEM(slots, f32),
            pltpu.VMEM(slots, f32),
            pltpu.VMEM(slots, bf16),
            pltpu.VMEM(slots, bf16),
            pltpu.VMEM(slots, bf16),
            pltpu.VMEM(slots, bf16),
            pltpu.VMEM(slots, bf16),
            pltpu.SemaphoreType.DMA((4, 2, chunks)),
            pltpu.SemaphoreType.DMA((4, 2, chunks)),
            pltpu.SemaphoreType.DMA((groups - 1, chunks)),
            pltpu.SemaphoreType.DMA((groups - 1, chunks)),
            pltpu.SemaphoreType.DMA((2, chunks)),
            pltpu.SemaphoreType.DMA((3, chunks)),
        ],
        compiler_params=pltpu.CompilerParams(
            collective_id=0, has_side_effects=True, vmem_limit_bytes=32 * 1024 * 1024
        ),
    )(query_bits, key_bits, values, grad_out)

    rows = CHUNK * query_bits.shape[0] // heads
    packed = pl.BlockSpec((rows, tokens), lambda j: (j, 0))
    wide = pl.BlockSpec((tokens, CHUNK * HD), lambda j: (0, j))
    result = jax.ShapeDtypeStruct((tokens, width), bf16)
    return pl.pallas_call(
        functools.partial(grads_kernel, att_scale),
        grid=(chunks,),
        out_shape=(result, result, result),
        in_specs=[
            pl.BlockSpec(memory_space=pltpu.SMEM),
            packed,
            packed,
            wide,
            wide,
            pl.BlockSpec((1, CHUNK, HD, HD), lambda j: (0, j, 0, 0)),
            pl.BlockSpec((1, CHUNK, HD, HD), lambda j: (1, j, 0, 0)),
        ],
        out_specs=(wide, wide, wide),
        compiler_params=pltpu.CompilerParams(vmem_limit_bytes=32 * 1024 * 1024),
    )(tile_mask, query_bits, key_bits, values, grad_heads, carry, carry)


def solution(mesh):
    return jax.shard_map(
        local,
        mesh=mesh,
        in_specs=(
            P("head", "ctx"),
            P("head", "ctx"),
            P("ctx", "head"),
            P("ctx", "head", None),
            P("ctx", None, None),
        ),
        out_specs=(P("ctx", "head"), P("ctx", "head"), P("ctx", "head")),
        check_vma=False,
    )
```

time: 434 us -> 91.2 us (0.21); the launches traced: 427 us -> 90.2 us
  waiting for transfers between devices: 197 us -> 0 us
  matrix products: 125 us -> 0 us
  Pallas kernels: 0 us -> 84.7 us
  other arithmetic: 49.1 us -> 0 us
  local copies, waits for them, and re-layouts: 23.1 us -> 4.92 us
  blocking collectives: 17.1 us -> 0 us
  between operations: 14.2 us -> 0.66 us
    all_gather x2 -> x0, waiting for transfers between devices: 197 us -> none  [carried_in(): gathered = lax.all_gather(part, axis)]
    dot_general x114 -> x0, matrix products: 125 us -> none  [the longest x16 30.8 us: stretch_grads(): jnp.dot(att_weights.T, grad_rows, preferred_element_type=jnp.float32)]
    pallas_call x0 -> x2, Pallas kernels: none -> 84.7 us  [the longest x1 78.2 us: local(): pl.pallas_call(functools.partial(scan_kernel, groups, stretches), out_sha...]
    unnamed x1 -> x0, other arithmetic: 23.4 us -> none
    add x15 -> x0, other arithmetic: 22.3 us -> none  [add_terms(): return earlier + later]
    all_to_all x1 -> x0, blocking collectives: 17.1 us -> none  [local(): lax.all_to_all(grad_out, 'head', split_axis=2, concat_axis=1, tiled=True)]
    unnamed x22 -> x10, local copies, waits for them, and re-layouts: 14.2 us -> 4.92 us
  transfers between devices with their start and end apart: 2 -> 0, of which waited for: 2 -> 0; matrix products, arithmetic and copies ran while one was open for 10% -> 0% of each run, Pallas kernels for 0% -> 0%
where the time goes in v1:
time: 91.2 us; the launch traced here: 90.2 us
  Pallas kernels  84.7 us (93%)
  local copies, waits for them, and re-layouts  4.92 us (5%)
    pallas_call x1, Pallas kernels, local(): pl.pallas_call(functools.partial(scan_kernel, groups, stretches), out_sha...  78.2 us
    pallas_call x1, Pallas kernels, local(): pl.pallas_call(functools.partial(grads_kernel, att_scale), grid=(chunks,)...  6.43 us
    unnamed x10, local copies, waits for them, and re-layouts  4.92 us

profile of v1, /device:TPU:1, one launch (start us, length us, event | category | flops | bytes accessed | tf_op | source)
XLA Modules:
  0.0 90.2 jit_solution(6584244113729479136)
XLA Ops:
  0.6 0.0 copy-start
  0.6 1.2 %copy-done = bf16[256,2048]{1,0:T(8,128)(2,1)S(1)} copy-done((bf16[256,2048]{1,0:T(8,128)(2,1)S(1)}, bf16[256,2048]{1,0:T(8,128)(2,1)}, u32[]{:S(2)}) %copy-start) | copy-done | bytes 1048600
  1.9 0.0 copy-start.1
  1.9 1.2 %copy-done.1 = bf16[1,128,4096]{2,1,0:T(8,128)(2,1)S(1)} copy-done((bf16[1,128,4096]{2,1,0:T(8,128)(2,1)S(1)}, bf16[1,128,4096]{2,1,0:T(8,128)(2,1)}, u32[]{:S(2)}) %copy-start.1) | copy-done | bytes 1048600
  3.1 0.0 copy-start.2
  3.1 0.9 copy-done.2
  4.0 0.0 copy-start.3
  4.0 0.9 copy-done.3
  4.9 78.2 %shard_map.76 = (bf16[2,16,128,128]{3,2,1,0:T(8,128)(2,1)S(1)}, bf16[256,2048]{1,0:T(8,128)(2,1)S(1)}) custom-call(s32[128,256]{1,0:T(8,128)S(1)} %copy-done.2, s32[128,256]{1,0:T(8,128)S(1)} %copy-done.3, bf16[256,2048]{1,0:T(8,128)(2,1)S(1)} %copy-done, bf16[1,128,4096]{2,1,0:T(8,128)(2,1)S(1)} %copy-done.1), custom_call_target="tpu_custom_call" | custom-call | tf_op jit(solution)/shard_map/pallas_call | solution.py:290
  83.1 0.0 copy-start.4
  83.2 0.7 copy-done.4
  83.8 6.4 %shard_map.77 = (bf16[256,2048]{1,0:T(8,128)(2,1)}, bf16[256,2048]{1,0:T(8,128)(2,1)}, bf16[256,2048]{1,0:T(8,128)(2,1)}) custom-call(s32[1,2,2]{2,1,0:T(2,128)S(1)} %copy-done.4, s32[128,256]{1,0:T(8,128)S(1)} %copy-done.2, s32[128,256]{1,0:T(8,128)S(1)} %copy-done.3, bf16[256,2048]{1,0:T(8,128)(2,1)S(1)} %copy-done, ...), custom_call_target="tpu_custom_call" | custom-call | tf_op jit(solution)/shard_map/pallas_call | solution.py:327
Async XLA Ops:
  0.6 1.2 %copy-start = (bf16[256,2048]{1,0:T(8,128)(2,1)S(1)}, bf16[256,2048]{1,0:T(8,128)(2,1)}, u32[]{:S(2)}) copy-start(bf16[256,2048]{1,0:T(8,128)(2,1)} %value_ref.1) | copy-start | bytes 3145732
  1.9 1.2 %copy-start.1 = (bf16[1,128,4096]{2,1,0:T(8,128)(2,1)S(1)}, bf16[1,128,4096]{2,1,0:T(8,128)(2,1)}, u32[]{:S(2)}) copy-start(bf16[1,128,4096]{2,1,0:T(8,128)(2,1)} %grad_hbm.1) | copy-start | bytes 3145732
  3.1 0.9 %copy-start.2 = (s32[128,256]{1,0:T(8,128)S(1)}, s32[128,256]{1,0:T(8,128)}, u32[]{:S(2)}) copy-start(s32[128,256]{1,0:T(8,128)} %query_ref.3) | copy-start | bytes 393220
  4.0 0.9 %copy-start.3 = (s32[128,256]{1,0:T(8,128)S(1)}, s32[128,256]{1,0:T(8,128)}, u32[]{:S(2)}) copy-start(s32[128,256]{1,0:T(8,128)} %key_ref.3) | copy-start | bytes 393220
  83.1 0.7 copy-start.4

commit v2 on v1

--- a/solution.py
+++ b/solution.py
@@ -9,8 +9,10 @@
 from jax.sharding import PartitionSpec as P
 
 HD = 128
-CHUNK = 4
+CHUNK = 2
 HALF = CHUNK // 2
+STEP = 4
+LAG = 2
 MESH = pl.DeviceIdType.MESH
 CORE, ROW, CHAIN, BACK = range(4)
 
@@ -25,11 +27,11 @@
 
 def scan_kernel(
     groups, stretches,
-    query_ref, key_ref, value_hbm, grad_hbm,
+    query_hbm, key_hbm, value_hbm, grad_hbm,
     carry_hbm, heads_hbm,
-    value_buf, grad_buf, carry, own, chip, core_out, core_in, row_out, row_in,
+    query_ref, key_ref, value_buf, grad_buf, carry, own, chip, core_out, core_in, row_out, row_in,
     chain_out, chain_in, back_out,
-    send_sem, recv_sem, swap_send, swap_recv, local_sem, out_sem,
+    send_sem, recv_sem, swap_send, swap_recv, local_sem, bits_sem, out_sem,
 ):
     tokens, width = value_buf.shape
     head_count = width // HD
@@ -75,7 +77,9 @@
         )
         for j in range(chunks)
     ]
-    for copy in value_in + grad_in:
+    key_in = pltpu.make_async_copy(key_hbm, key_ref, bits_sem.at[0])
+    query_in = pltpu.make_async_copy(query_hbm, query_ref, bits_sem.at[1])
+    for copy in [key_in] + value_in + [query_in] + grad_in:
         copy.start()
 
     pl.semaphore_wait(
@@ -199,19 +203,28 @@
         back_copy(which, j).wait_recv()
         carry_out(which, j).start()
 
+    def chain_slot(which, j):
+        @pl.when((j >= 0) & (j < chunks))
+        def _():
+            chain(which, j)
+
+    key_in.wait()
     for j in range(chunks + 1):
         if j < chunks:
             terms(0, j)
         if j > 0:
             chip_sum(0, j - 1)
-    for j in range(chunks + 1):
-        if j < chunks:
-            terms(1, j)
-            heads_out(j).start()
-            chain(0, j)
-            chip_sum(1, j)
-        if j > 0:
-            chain(1, j - 1)
+    query_in.wait()
+    for slot in range(LAG + chunks + planes - 1):
+        if slot < chunks:
+            terms(1, slot)
+            heads_out(slot).start()
+        if slot < chunks + planes - 1:
+            chain_slot(0, slot - plane)
+        if 0 < slot <= chunks:
+            chip_sum(1, slot - 1)
+        if slot >= LAG:
+            chain_slot(1, slot - LAG - (planes - 1 - plane))
     for which in range(2):
         for j in range(chunks):
             land(which, j)
@@ -238,7 +251,7 @@
     query_out, key_out, value_out,
 ):
     tokens = value_ref.shape[0]
-    words = query_ref.shape[0] // CHUNK
+    words = query_ref.shape[0] // STEP
     tile_count = tiles_ref.shape[1]
     size = tokens // tile_count
     t = lax.broadcasted_iota(jnp.int32, (tokens, tokens), 0)
@@ -258,7 +271,7 @@
         return lax.dot_general(a, b, (dims, ((), ())), preferred_element_type=jnp.float32)
 
     last = ((1,), (1,))
-    for i in range(CHUNK):
+    for i in range(STEP):
         columns = slice(i * HD, (i + 1) * HD)
         query = spikes(query_ref, i, words)
         key_t = spikes(key_ref, i, words).T
@@ -286,16 +299,18 @@
     att_scale = 4.0 / (HD * math.sqrt(tokens * stretches))
     bf16, f32 = jnp.bfloat16, jnp.float32
     slots = (2, chunks, HALF, HD, HD)
-    vmem, any_space = pl.BlockSpec(memory_space=pltpu.VMEM), pl.BlockSpec(memory_space=pl.ANY)
+    hbm = pl.BlockSpec(memory_space=pltpu.HBM)
     carry, grad_heads = pl.pallas_call(
         functools.partial(scan_kernel, groups, stretches),
         out_shape=(
             jax.ShapeDtypeStruct((2, heads, HD, HD), bf16),
             jax.ShapeDtypeStruct((tokens, width), bf16),
         ),
-        in_specs=[vmem, vmem, any_space, any_space],
-        out_specs=(any_space, any_space),
+        in_specs=[hbm, hbm, hbm, hbm],
+        out_specs=(hbm, hbm),
         scratch_shapes=[
+            pltpu.VMEM(query_bits.shape, jnp.int32),
+            pltpu.VMEM(key_bits.shape, jnp.int32),
             pltpu.VMEM((tokens, width), bf16),
             pltpu.VMEM((tokens, width), bf16),
             pltpu.VMEM((2, heads, HD, HD), bf16),
@@ -313,20 +328,21 @@
             pltpu.SemaphoreType.DMA((groups - 1, chunks)),
             pltpu.SemaphoreType.DMA((groups - 1, chunks)),
             pltpu.SemaphoreType.DMA((2, chunks)),
+            pltpu.SemaphoreType.DMA((2,)),
             pltpu.SemaphoreType.DMA((3, chunks)),
         ],
         compiler_params=pltpu.CompilerParams(
-            collective_id=0, has_side_effects=True, vmem_limit_bytes=32 * 1024 * 1024
+            collective_id=0, has_side_effects=True, vmem_limit_bytes=63 * 1024 * 1024
         ),
     )(query_bits, key_bits, values, grad_out)
 
-    rows = CHUNK * query_bits.shape[0] // heads
+    rows = STEP * query_bits.shape[0] // heads
     packed = pl.BlockSpec((rows, tokens), lambda j: (j, 0))
-    wide = pl.BlockSpec((tokens, CHUNK * HD), lambda j: (0, j))
+    wide = pl.BlockSpec((tokens, STEP * HD), lambda j: (0, j))
     result = jax.ShapeDtypeStruct((tokens, width), bf16)
     return pl.pallas_call(
         functools.partial(grads_kernel, att_scale),
-        grid=(chunks,),
+        grid=(heads // STEP,),
         out_shape=(result, result, result),
         in_specs=[
             pl.BlockSpec(memory_space=pltpu.SMEM),
@@ -334,11 +350,11 @@
             packed,
             wide,
             wide,
-            pl.BlockSpec((1, CHUNK, HD, HD), lambda j: (0, j, 0, 0)),
-            pl.BlockSpec((1, CHUNK, HD, HD), lambda j: (1, j, 0, 0)),
+            pl.BlockSpec((1, STEP, HD, HD), lambda j: (0, j, 0, 0)),
+            pl.BlockSpec((1, STEP, HD, HD), lambda j: (1, j, 0, 0)),
         ],
         out_specs=(wide, wide, wide),
-        compiler_params=pltpu.CompilerParams(vmem_limit_bytes=32 * 1024 * 1024),
+        compiler_params=pltpu.CompilerParams(vmem_limit_bytes=63 * 1024 * 1024),
     )(tile_mask, query_bits, key_bits, values, grad_heads, carry, carry)
 
 

time: 91.2 us -> 52.5 us (0.58)
  Pallas kernels: 84.7 us -> 51.7 us
  local copies, waits for them, and re-layouts: 4.92 us -> 0 us
    pallas_call x1, Pallas kernels: 78.2 us -> 44.7 us  [local(): pl.pallas_call(functools.partial(scan_kernel, groups, stretches), out_sha...]
    unnamed x10 -> x0, local copies, waits for them, and re-layouts: 4.92 us -> none
where the time goes in v2:
time: 52.5 us; the launch traced here: 52.3 us
  Pallas kernels  51.7 us (98%)
  between operations  0.64 us (1%)
    pallas_call x1, Pallas kernels, local(): pl.pallas_call(functools.partial(scan_kernel, groups, stretches), out_sha...  44.7 us
    pallas_call x1, Pallas kernels, local(): pl.pallas_call(functools.partial(grads_kernel, att_scale), grid=(heads //...  7 us

profile of v2, /device:TPU:1, one launch (start us, length us, event | category | flops | bytes accessed | tf_op | source)
XLA Modules:
  0.0 52.3 jit_solution(2125382141517896423)
XLA Ops:
  0.6 44.7 %shard_map.76 = (bf16[2,16,128,128]{3,2,1,0:T(8,128)(2,1)}, bf16[256,2048]{1,0:T(8,128)(2,1)}) custom-call(s32[128,256]{1,0:T(8,128)} %query_ref.1, s32[128,256]{1,0:T(8,128)} %key_ref.1, bf16[256,2048]{1,0:T(8,128)(2,1)} %value_ref.1, bf16[1,128,4096]{2,1,0:T(8,128)(2,1)} %grad_hbm.1), custom_call_target="tpu_custom_call" | custom-call | tf_op jit(solution)/shard_map/pallas_call | solution.py:303
  45.3 7.0 %shard_map.77 = (bf16[256,2048]{1,0:T(8,128)(2,1)}, bf16[256,2048]{1,0:T(8,128)(2,1)}, bf16[256,2048]{1,0:T(8,128)(2,1)}) custom-call(s32[1,2,2]{2,1,0:T(2,128)} %tiles_ref.1, s32[128,256]{1,0:T(8,128)} %query_ref.1, s32[128,256]{1,0:T(8,128)} %key_ref.1, bf16[256,2048]{1,0:T(8,128)(2,1)} %value_ref.1, bf16[256,2048]{1,0:T(8,128)(2,1)} %get-tuple-element.5.grad_ref, ...), custom_call_target="tpu_custom_call" | custom-call | tf_op jit(solution)/shard_map/pallas_call | solution.py:343

commit v3 on v2

--- a/solution.py
+++ b/solution.py
@@ -11,8 +11,7 @@
 HD = 128
 CHUNK = 2
 HALF = CHUNK // 2
-STEP = 4
-LAG = 2
+LAG = 1
 MESH = pl.DeviceIdType.MESH
 CORE, ROW, CHAIN, BACK = range(4)
 
@@ -26,10 +25,11 @@
 
 
 def scan_kernel(
-    groups, stretches,
-    query_hbm, key_hbm, value_hbm, grad_hbm,
-    carry_hbm, heads_hbm,
-    query_ref, key_ref, value_buf, grad_buf, carry, own, chip, core_out, core_in, row_out, row_in,
+    groups, stretches, att_scale,
+    tiles_ref, query_hbm, key_hbm, value_hbm, grad_hbm,
+    query_out, key_out, value_out,
+    query_ref, key_ref, query_spk, key_spk, key_rows, keep, keep_t,
+    query_part, key_part, value_part, query_buf, key_buf, result_buf, value_buf, grad_buf, carry, own, chip, core_out, core_in, row_out, row_in,
     chain_out, chain_in, back_out,
     send_sem, recv_sem, swap_send, swap_recv, local_sem, bits_sem, out_sem,
 ):
@@ -82,6 +82,25 @@
     for copy in [key_in] + value_in + [query_in] + grad_in:
         copy.start()
 
+    tile_count = tiles_ref.shape[1]
+    size = tokens // tile_count
+    down = lax.broadcasted_iota(jnp.int32, (tokens, tokens), 0)
+    along = lax.broadcasted_iota(jnp.int32, (tokens, tokens), 1)
+
+    def masked(t, s):
+        mask = jnp.where((t >= s) & (t // size == s // size), att_scale, 0.0)
+        for later in range(tile_count):
+            for earlier in range(later):
+                allowed = tiles_ref[0, later, earlier].astype(jnp.float32) * att_scale
+                mask = jnp.where((t // size == later) & (s // size == earlier), allowed, mask)
+        return mask
+
+    keep[...] = masked(down, along)
+    keep_t[...] = masked(along, down)
+    key_in.wait()
+    for head in range(head_count):
+        key_spk[head] = spikes(key_ref, head, words)
+
     pl.semaphore_wait(
         barrier, groups + 1 + has_above.astype(jnp.int32) + has_below.astype(jnp.int32)
     )
@@ -142,10 +161,10 @@
         dots = []
         for head in range(j * CHUNK, (j + 1) * CHUNK):
             rows = value_buf if which == 0 else grad_buf
-            spike = spikes(key_ref if which == 0 else query_ref, head, words)
+            spike = key_spk if which == 0 else query_spk
             dots.append(
                 jnp.dot(
-                    spike, rows[:, head * HD : (head + 1) * HD], preferred_element_type=jnp.float32
+                    spike[head], rows[:, head * HD : (head + 1) * HD], preferred_element_type=jnp.float32
                 )
             )
         for i in range(HALF):
@@ -188,51 +207,103 @@
         back_copy(which, j).start()
         carry[which, mine(j)] = jnp.where(nearer, base, more).astype(jnp.bfloat16)
 
-    def carry_out(which, j):
-        heads = pl.ds(j * CHUNK, CHUNK)
+    def dot(x, y, dims=((1,), (0,))):
+        return lax.dot_general(x, y, (dims, ((), ())), preferred_element_type=jnp.float32)
+
+    last = ((1,), (1,))
+
+    def lanes(head):
+        return slice(head * HD, (head + 1) * HD)
+
+    def heads_of(j):
+        return range(j * CHUNK, (j + 1) * CHUNK)
+
+    def within(j):
+        for head in heads_of(j):
+            query = query_spk[head]
+            rows = key_rows[head]
+            value = value_buf[:, lanes(head)]
+            grad = grad_buf[:, lanes(head)]
+            weights = (dot(grad, value, last) * keep[...]).astype(jnp.bfloat16)
+            query_part[:, lanes(head)] = dot(weights, rows)
+            weights_t = (dot(value, grad, last) * keep_t[...]).astype(jnp.bfloat16)
+            key_part[:, lanes(head)] = dot(weights_t, query, last)
+            att_t = (dot(rows, query) * keep_t[...]).astype(jnp.bfloat16)
+            value_part[:, lanes(head)] = dot(att_t, grad)
+
+    def result_copy(kind, j):
+        source = (query_buf, key_buf, result_buf)[kind]
+        target = (query_out, key_out, value_out)[kind]
         return pltpu.make_async_copy(
-            carry.at[which, heads], carry_hbm.at[which, heads], out_sem.at[which, j]
+            source.at[:, cols(j)], target.at[:, cols(j)], out_sem.at[kind, j]
         )
 
-    def heads_out(j):
-        return pltpu.make_async_copy(
-            grad_buf.at[:, cols(j)], heads_hbm.at[:, cols(j)], out_sem.at[2, j]
-        )
-
-    def land(which, j):
-        back_copy(which, j).wait_recv()
-        carry_out(which, j).start()
+    def finish_query(j):
+        back_copy(0, j).wait_recv()
+        for head in heads_of(j):
+            across_part = dot(grad_buf[:, lanes(head)], carry[0, head], last)
+            query_buf[:, lanes(head)] = (
+                query_part[:, lanes(head)] + att_scale * across_part
+            ).astype(jnp.bfloat16)
+        result_copy(0, j).start()
+
+    def finish_key_value(j):
+        back_copy(1, j).wait_recv()
+        for head in heads_of(j):
+            adjoint = carry[1, head]
+            key_buf[:, lanes(head)] = (
+                key_part[:, lanes(head)]
+                + att_scale * dot(value_buf[:, lanes(head)], adjoint, last)
+            ).astype(jnp.bfloat16)
+            result_buf[:, lanes(head)] = (
+                value_part[:, lanes(head)] + att_scale * dot(key_rows[head], adjoint)
+            ).astype(jnp.bfloat16)
+        result_copy(1, j).start()
+        result_copy(2, j).start()
 
     def chain_slot(which, j):
         @pl.when((j >= 0) & (j < chunks))
         def _():
             chain(which, j)
 
-    key_in.wait()
     for j in range(chunks + 1):
         if j < chunks:
             terms(0, j)
         if j > 0:
             chip_sum(0, j - 1)
     query_in.wait()
-    for slot in range(LAG + chunks + planes - 1):
+    for head in range(head_count):
+        query_spk[head] = spikes(query_ref, head, words)
+        key_rows[head] = key_spk[head].T
+
+    state_slots = chunks + planes - 1
+    asked = 0
+    done = 0
+    for slot in range(LAG + chunks + planes):
         if slot < chunks:
             terms(1, slot)
-            heads_out(slot).start()
-        if slot < chunks + planes - 1:
-            chain_slot(0, slot - plane)
+        ahead = min(2 * slot + 2, state_slots) if slot < chunks else state_slots
+        for early in range(asked, ahead):
+            chain_slot(0, early - plane)
+        asked = ahead
         if 0 < slot <= chunks:
-            chip_sum(1, slot - 1)
-        if slot >= LAG:
+            within(slot - 1)
+        if slot < chunks:
+            chip_sum(1, slot)
+        if LAG <= slot < LAG + state_slots:
             chain_slot(1, slot - LAG - (planes - 1 - plane))
-    for which in range(2):
-        for j in range(chunks):
-            land(which, j)
+        ready = min(max(asked - planes, 0), slot, chunks)
+        for j in range(done, ready):
+            finish_query(j)
+        done = ready
+        if slot >= LAG + planes:
+            finish_key_value(slot - LAG - planes)
+    for j in range(done, chunks):
+        finish_query(j)
 
     for j in range(chunks):
         for copy in swaps[j]:
             copy.wait_send()
-        heads_out(j).wait()
         for which in range(2):
             core_copy(which, j).wait_send()
             row_copy(which, j).wait_send()
@@ -242,53 +313,8 @@
             def _():
                 chain_copy(which, j).wait_send()
 
-            carry_out(which, j).wait()
-
-
-def grads_kernel(
-    att_scale,
-    tiles_ref, query_ref, key_ref, value_ref, grad_ref, state_ref, adjoint_ref,
-    query_out, key_out, value_out,
-):
-    tokens = value_ref.shape[0]
-    words = query_ref.shape[0] // STEP
-    tile_count = tiles_ref.shape[1]
-    size = tokens // tile_count
-    t = lax.broadcasted_iota(jnp.int32, (tokens, tokens), 0)
-    s = lax.broadcasted_iota(jnp.int32, (tokens, tokens), 1)
-
-    def masked(t, s):
-        keep = jnp.where((t >= s) & (t // size == s // size), att_scale, 0.0)
-        for a in range(tile_count):
-            for b in range(a):
-                allowed = tiles_ref[0, a, b].astype(jnp.float32) * att_scale
-                keep = jnp.where((t // size == a) & (s // size == b), allowed, keep)
-        return keep
-
-    keep, keep_t = masked(t, s), masked(s, t)
-
-    def dot(a, b, dims=((1,), (0,))):
-        return lax.dot_general(a, b, (dims, ((), ())), preferred_element_type=jnp.float32)
-
-    last = ((1,), (1,))
-    for i in range(STEP):
-        columns = slice(i * HD, (i + 1) * HD)
-        query = spikes(query_ref, i, words)
-        key_t = spikes(key_ref, i, words).T
-        value = value_ref[:, columns]
-        grad = grad_ref[:, columns]
-        weights = (dot(grad, value, last) * keep).astype(jnp.bfloat16)
-        weights_t = (dot(value, grad, last) * keep_t).astype(jnp.bfloat16)
-        att_t = (dot(key_t, query) * keep_t).astype(jnp.bfloat16)
-        query_out[:, columns] = (
-            dot(weights, key_t) + att_scale * dot(grad, state_ref[0, i], last)
-        ).astype(jnp.bfloat16)
-        key_out[:, columns] = (
-            dot(weights_t, query, last) + att_scale * dot(value, adjoint_ref[0, i], last)
-        ).astype(jnp.bfloat16)
-        value_out[:, columns] = (
-            dot(att_t, grad) + att_scale * dot(key_t, adjoint_ref[0, i])
-        ).astype(jnp.bfloat16)
+        for kind in range(3):
+            result_copy(kind, j).wait()
 
 
 def local(query_bits, key_bits, values, grad_out, tile_mask):
@@ -300,17 +326,27 @@
     bf16, f32 = jnp.bfloat16, jnp.float32
     slots = (2, chunks, HALF, HD, HD)
     hbm = pl.BlockSpec(memory_space=pltpu.HBM)
-    carry, grad_heads = pl.pallas_call(
-        functools.partial(scan_kernel, groups, stretches),
-        out_shape=(
-            jax.ShapeDtypeStruct((2, heads, HD, HD), bf16),
-            jax.ShapeDtypeStruct((tokens, width), bf16),
-        ),
-        in_specs=[hbm, hbm, hbm, hbm],
-        out_specs=(hbm, hbm),
+    spk, wide = (heads, HD, tokens), (tokens, width)
+    result = jax.ShapeDtypeStruct(wide, bf16)
+    return pl.pallas_call(
+        functools.partial(scan_kernel, groups, stretches, att_scale),
+        out_shape=(result, result, result),
+        in_specs=[pl.BlockSpec(memory_space=pltpu.SMEM), hbm, hbm, hbm, hbm],
+        out_specs=(hbm, hbm, hbm),
         scratch_shapes=[
             pltpu.VMEM(query_bits.shape, jnp.int32),
             pltpu.VMEM(key_bits.shape, jnp.int32),
+            pltpu.VMEM(spk, bf16),
+            pltpu.VMEM(spk, bf16),
+            pltpu.VMEM((heads, tokens, HD), bf16),
+            pltpu.VMEM((tokens, tokens), f32),
+            pltpu.VMEM((tokens, tokens), f32),
+            pltpu.VMEM(wide, f32),
+            pltpu.VMEM(wide, f32),
+            pltpu.VMEM(wide, f32),
+            pltpu.VMEM(wide, bf16),
+            pltpu.VMEM(wide, bf16),
+            pltpu.VMEM(wide, bf16),
             pltpu.VMEM((tokens, width), bf16),
             pltpu.VMEM((tokens, width), bf16),
             pltpu.VMEM((2, heads, HD, HD), bf16),
@@ -334,28 +370,7 @@
         compiler_params=pltpu.CompilerParams(
             collective_id=0, has_side_effects=True, vmem_limit_bytes=63 * 1024 * 1024
         ),
-    )(query_bits, key_bits, values, grad_out)
-
-    rows = STEP * query_bits.shape[0] // heads
-    packed = pl.BlockSpec((rows, tokens), lambda j: (j, 0))
-    wide = pl.BlockSpec((tokens, STEP * HD), lambda j: (0, j))
-    result = jax.ShapeDtypeStruct((tokens, width), bf16)
-    return pl.pallas_call(
-        functools.partial(grads_kernel, att_scale),
-        grid=(heads // STEP,),
-        out_shape=(result, result, result),
-        in_specs=[
-            pl.BlockSpec(memory_space=pltpu.SMEM),
-            packed,
-            packed,
-            wide,
-            wide,
-            pl.BlockSpec((1, STEP, HD, HD), lambda j: (0, j, 0, 0)),
-            pl.BlockSpec((1, STEP, HD, HD), lambda j: (1, j, 0, 0)),
-        ],
-        out_specs=(wide, wide, wide),
-        compiler_params=pltpu.CompilerParams(vmem_limit_bytes=63 * 1024 * 1024),
-    )(tile_mask, query_bits, key_bits, values, grad_heads, carry, carry)
+    )(tile_mask, query_bits, key_bits, values, grad_out)
 
 
 def solution(mesh):

time: 52.5 us -> 57.5 us (1.095)
  local copies, waits for them, and re-layouts: 0 us -> 4.97 us
    unnamed x0 -> x7, local copies, waits for them, and re-layouts: none -> 4.97 us
    pallas_call x2 -> x1, Pallas kernels: 51.7 us -> 51.6 us  [local(): pl.pallas_call(functools.partial(scan_kernel, groups, stretches, att_scal...]
where the time goes in v3:
time: 57.5 us; the launch traced here: 57.2 us
  Pallas kernels  51.6 us (90%)
  local copies, waits for them, and re-layouts  4.97 us (9%)
  between operations  0.65 us (1%)
    pallas_call x1, Pallas kernels, local(): pl.pallas_call(functools.partial(scan_kernel, groups, stretches, att_scal...  51.6 us
    unnamed x7, local copies, waits for them, and re-layouts  4.97 us

profile of v3, /device:TPU:1, one launch (start us, length us, event | category | flops | bytes accessed | tf_op | source)
XLA Modules:
  0.0 57.2 jit_solution(6365566336792398333)
XLA Ops:
  0.6 51.6 %shard_map.76 = (bf16[256,2048]{1,0:T(8,128)(2,1)}, bf16[256,2048]{1,0:T(8,128)(2,1)}, bf16[256,2048]{1,0:T(8,128)(2,1)}) custom-call(s32[1,2,2]{2,1,0:T(2,128)} %tiles_ref.1, s32[128,256]{1,0:T(8,128)} %query_hbm.1, s32[128,256]{1,0:T(8,128)} %key_hbm.1, bf16[256,2048]{1,0:T(8,128)(2,1)} %value_hbm.1, bf16[1,128,4096]{2,1,0:T(8,128)(2,1)} %grad_hbm.1), custom_call_target="tpu_custom_call" | custom-call | tf_op jit(solution)/shard_map/pallas_call | solution.py:331
  52.3 0.0 copy-start.1
  52.3 2.4 %copy.11 = bf16[256,2048]{1,0:T(8,128)(2,1)} copy(bf16[256,2048]{1,0:T(8,128)(2,1)} %get-tuple-element.6) | data formatting | bytes 2097152
  54.7 0.0 copy-done.1
  54.7 0.0 copy-start
  54.7 1.0 %copy.12 = bf16[256,2048]{1,0:T(8,128)(2,1)} copy(bf16[256,2048]{1,0:T(8,128)(2,1)S(1)} %copy-done.1) | data formatting | bytes 2097152
  55.6 0.6 %copy-done = bf16[256,2048]{1,0:T(8,128)(2,1)S(1)} copy-done((bf16[256,2048]{1,0:T(8,128)(2,1)S(1)}, bf16[256,2048]{1,0:T(8,128)(2,1)}, u32[]{:S(2)}) %copy-start) | copy-done | bytes 1048600
  56.3 1.0 %copy.13 = bf16[256,2048]{1,0:T(8,128)(2,1)} copy(bf16[256,2048]{1,0:T(8,128)(2,1)S(1)} %copy-done) | data formatting | bytes 2097152
Async XLA Ops:
  52.3 2.4 %copy-start.1 = (bf16[256,2048]{1,0:T(8,128)(2,1)S(1)}, bf16[256,2048]{1,0:T(8,128)(2,1)}, u32[]{:S(2)}) copy-start(bf16[256,2048]{1,0:T(8,128)(2,1)} %get-tuple-element.7) | copy-start | bytes 3145732
  54.7 1.6 %copy-start = (bf16[256,2048]{1,0:T(8,128)(2,1)S(1)}, bf16[256,2048]{1,0:T(8,128)(2,1)}, u32[]{:S(2)}) copy-start(bf16[256,2048]{1,0:T(8,128)(2,1)} %get-tuple-element.8) | copy-start | bytes 3145732

commit v4 on v3

--- a/solution.py
+++ b/solution.py
@@ -11,7 +11,10 @@
 HD = 128
 CHUNK = 2
 HALF = CHUNK // 2
-LAG = 1
+LAG = 3
+SKEW = 2
+STATE_SKEW = 4
+PIECES = 4
 MESH = pl.DeviceIdType.MESH
 CORE, ROW, CHAIN, BACK = range(4)
 
@@ -266,38 +269,40 @@
         def _():
             chain(which, j)
 
-    for j in range(chunks + 1):
-        if j < chunks:
-            terms(0, j)
-        if j > 0:
-            chip_sum(0, j - 1)
+    for j in range(chunks):
+        terms(0, j)
     query_in.wait()
     for head in range(head_count):
         query_spk[head] = spikes(query_ref, head, words)
         key_rows[head] = key_spk[head].T
-
-    state_slots = chunks + planes - 1
-    asked = 0
-    done = 0
-    for slot in range(LAG + chunks + planes):
+    for j in range(chunks):
+        chip_sum(0, j)
+
+    span = planes - 1
+    state_slots = chunks + STATE_SKEW * span
+    slots = LAG + chunks + SKEW * span
+    asked = done = 0
+    for slot in range(slots + 2):
         if slot < chunks:
             terms(1, slot)
-        ahead = min(2 * slot + 2, state_slots) if slot < chunks else state_slots
+        ahead = min(2 * slot, state_slots)
         for early in range(asked, ahead):
-            chain_slot(0, early - plane)
+            chain_slot(0, early - STATE_SKEW * plane)
         asked = ahead
         if 0 < slot <= chunks:
+            chip_sum(1, slot - 1)
+        if LAG <= slot < slots:
+            chain_slot(1, slot - LAG - SKEW * (span - plane))
+        if 0 < slot <= chunks:
             within(slot - 1)
-        if slot < chunks:
-            chip_sum(1, slot)
-        if LAG <= slot < LAG + state_slots:
-            chain_slot(1, slot - LAG - (planes - 1 - plane))
-        ready = min(max(asked - planes, 0), slot, chunks)
+        ready = min(max(asked - STATE_SKEW * span - 2, 0), slot, chunks)
         for j in range(done, ready):
             finish_query(j)
-        done = ready
-        if slot >= LAG + planes:
-            finish_key_value(slot - LAG - planes)
+        done = max(done, ready)
+        if slot >= slots + 2 - chunks:
+            finish_key_value(slot - (slots + 2 - chunks))
+    for early in range(asked, state_slots):
+        chain_slot(0, early - STATE_SKEW * plane)
     for j in range(done, chunks):
         finish_query(j)
 
@@ -315,6 +320,29 @@
 
         for kind in range(3):
             result_copy(kind, j).wait()
+
+
+def place_kernel(query_in, key_in, value_in, query_out, key_out, value_out, held, sem):
+    rows = held.shape[1] // PIECES
+    inward, outward = [], []
+    for kind, (source, target) in enumerate(
+        ((query_in, query_out), (key_in, key_out), (value_in, value_out))
+    ):
+        for piece in range(PIECES):
+            part = pl.ds(piece * rows, rows)
+            inward.append(
+                pltpu.make_async_copy(source.at[part], held.at[kind, part], sem.at[0, kind, piece])
+            )
+            outward.append(
+                pltpu.make_async_copy(held.at[kind, part], target.at[part], sem.at[1, kind, piece])
+            )
+    for copy in inward:
+        copy.start()
+    for arrived, leaving in zip(inward, outward):
+        arrived.wait()
+        leaving.start()
+    for copy in outward:
+        copy.wait()
 
 
 def local(query_bits, key_bits, values, grad_out, tile_mask):
@@ -328,7 +356,7 @@
     hbm = pl.BlockSpec(memory_space=pltpu.HBM)
     spk, wide = (heads, HD, tokens), (tokens, width)
     result = jax.ShapeDtypeStruct(wide, bf16)
-    return pl.pallas_call(
+    results = pl.pallas_call(
         functools.partial(scan_kernel, groups, stretches, att_scale),
         out_shape=(result, result, result),
         in_specs=[pl.BlockSpec(memory_space=pltpu.SMEM), hbm, hbm, hbm, hbm],
@@ -371,6 +399,17 @@
             collective_id=0, has_side_effects=True, vmem_limit_bytes=63 * 1024 * 1024
         ),
     )(tile_mask, query_bits, key_bits, values, grad_out)
+    return pl.pallas_call(
+        place_kernel,
+        out_shape=(result, result, result),
+        in_specs=[hbm, hbm, hbm],
+        out_specs=(hbm, hbm, hbm),
+        scratch_shapes=[
+            pltpu.VMEM((3, *wide), bf16),
+            pltpu.SemaphoreType.DMA((2, 3, PIECES)),
+        ],
+        compiler_params=pltpu.CompilerParams(vmem_limit_bytes=63 * 1024 * 1024),
+    )(*results)
 
 
 def solution(mesh):

time: 57.5 us -> 42.3 us (0.74)
  Pallas kernels: 51.6 us -> 41.5 us
  local copies, waits for them, and re-layouts: 4.97 us -> 0 us
    pallas_call x1, Pallas kernels: 51.6 us -> 38.6 us  [local(): pl.pallas_call(functools.partial(scan_kernel, groups, stretches, att_scal...]
    unnamed x7 -> x0, local copies, waits for them, and re-layouts: 4.97 us -> none
    pallas_call x0 -> x1, Pallas kernels: none -> 2.81 us  [local(): pl.pallas_call(place_kernel, out_shape=(result, result, result), in_specs...]
where the time goes in v4:
time: 42.3 us; the launch traced here: 42.1 us
  Pallas kernels  41.5 us (98%)
  between operations  0.64 us (2%)
    pallas_call x1, Pallas kernels, local(): pl.pallas_call(functools.partial(scan_kernel, groups, stretches, att_scal...  38.6 us
    pallas_call x1, Pallas kernels, local(): pl.pallas_call(place_kernel, out_shape=(result, result, result), in_specs...  2.81 us

profile of v4, /device:TPU:1, one launch (start us, length us, event | category | flops | bytes accessed | tf_op | source)
XLA Modules:
  0.0 42.1 jit_solution(2563851552166611681)
XLA Ops:
  0.6 38.6 %shard_map.76 = (bf16[256,2048]{1,0:T(8,128)(2,1)}, bf16[256,2048]{1,0:T(8,128)(2,1)}, bf16[256,2048]{1,0:T(8,128)(2,1)}) custom-call(s32[1,2,2]{2,1,0:T(2,128)} %tiles_ref.1, s32[128,256]{1,0:T(8,128)} %query_hbm.1, s32[128,256]{1,0:T(8,128)} %key_hbm.1, bf16[256,2048]{1,0:T(8,128)(2,1)} %value_hbm.1, bf16[1,128,4096]{2,1,0:T(8,128)(2,1)} %grad_hbm.1), custom_call_target="tpu_custom_call" | custom-call | tf_op jit(solution)/shard_map/pallas_call | solution.py:359
  39.3 2.8 %shard_map.77 = (bf16[256,2048]{1,0:T(8,128)(2,1)}, bf16[256,2048]{1,0:T(8,128)(2,1)}, bf16[256,2048]{1,0:T(8,128)(2,1)}) custom-call(bf16[256,2048]{1,0:T(8,128)(2,1)} %get-tuple-element.6.query_in, bf16[256,2048]{1,0:T(8,128)(2,1)} %get-tuple-element.7.key_in, bf16[256,2048]{1,0:T(8,128)(2,1)} %get-tuple-element.8.value_in), custom_call_target="tpu_custom_call" | custom-call | tf_op jit(solution)/shard_map/pallas_call | solution.py:402

commit v5 on v4

--- a/solution.py
+++ b/solution.py
@@ -85,25 +85,6 @@
     for copy in [key_in] + value_in + [query_in] + grad_in:
         copy.start()
 
-    tile_count = tiles_ref.shape[1]
-    size = tokens // tile_count
-    down = lax.broadcasted_iota(jnp.int32, (tokens, tokens), 0)
-    along = lax.broadcasted_iota(jnp.int32, (tokens, tokens), 1)
-
-    def masked(t, s):
-        mask = jnp.where((t >= s) & (t // size == s // size), att_scale, 0.0)
-        for later in range(tile_count):
-            for earlier in range(later):
-                allowed = tiles_ref[0, later, earlier].astype(jnp.float32) * att_scale
-                mask = jnp.where((t // size == later) & (s // size == earlier), allowed, mask)
-        return mask
-
-    keep[...] = masked(down, along)
-    keep_t[...] = masked(along, down)
-    key_in.wait()
-    for head in range(head_count):
-        key_spk[head] = spikes(key_ref, head, words)
-
     pl.semaphore_wait(
         barrier, groups + 1 + has_above.astype(jnp.int32) + has_below.astype(jnp.int32)
     )
@@ -125,6 +106,25 @@
     for copies in swaps:
         for copy in copies:
             copy.start()
+
+    tile_count = tiles_ref.shape[1]
+    size = tokens // tile_count
+    down = lax.broadcasted_iota(jnp.int32, (tokens, tokens), 0)
+    along = lax.broadcasted_iota(jnp.int32, (tokens, tokens), 1)
+
+    def masked(t, s):
+        mask = jnp.where((t >= s) & (t // size == s // size), att_scale, 0.0)
+        for later in range(tile_count):
+            for earlier in range(later):
+                allowed = tiles_ref[0, later, earlier].astype(jnp.float32) * att_scale
+                mask = jnp.where((t // size == later) & (s // size == earlier), allowed, mask)
+        return mask
+
+    keep[...] = masked(down, along)
+    keep_t[...] = masked(along, down)
+    key_in.wait()
+    for head in range(head_count):
+        key_spk[head] = spikes(key_ref, head, words)
 
     def remote(kind, which, j, src, dst, device):
         return pltpu.make_async_remote_copy(

time: 42.3 us -> 42.5 us (level)
  no operation moved by 1% of the time
where the time goes in v5:
time: 42.5 us; the launch traced here: 42.4 us
  Pallas kernels  41.7 us (98%)
  between operations  0.64 us (2%)
    pallas_call x1, Pallas kernels, local(): pl.pallas_call(functools.partial(scan_kernel, groups, stretches, att_scal...  38.9 us
    pallas_call x1, Pallas kernels, local(): pl.pallas_call(place_kernel, out_shape=(result, result, result), in_specs...  2.81 us

profile of v5, /device:TPU:1, one launch (start us, length us, event | category | flops | bytes accessed | tf_op | source)
XLA Modules:
  0.0 42.4 jit_solution(10521974897365452321)
XLA Ops:
  0.6 38.9 %shard_map.76 = (bf16[256,2048]{1,0:T(8,128)(2,1)}, bf16[256,2048]{1,0:T(8,128)(2,1)}, bf16[256,2048]{1,0:T(8,128)(2,1)}) custom-call(s32[1,2,2]{2,1,0:T(2,128)} %tiles_ref.1, s32[128,256]{1,0:T(8,128)} %query_hbm.1, s32[128,256]{1,0:T(8,128)} %key_hbm.1, bf16[256,2048]{1,0:T(8,128)(2,1)} %value_hbm.1, bf16[1,128,4096]{2,1,0:T(8,128)(2,1)} %grad_hbm.1), custom_call_target="tpu_custom_call" | custom-call | tf_op jit(solution)/shard_map/pallas_call | solution.py:359
  39.5 2.8 %shard_map.77 = (bf16[256,2048]{1,0:T(8,128)(2,1)}, bf16[256,2048]{1,0:T(8,128)(2,1)}, bf16[256,2048]{1,0:T(8,128)(2,1)}) custom-call(bf16[256,2048]{1,0:T(8,128)(2,1)} %get-tuple-element.6.query_in, bf16[256,2048]{1,0:T(8,128)(2,1)} %get-tuple-element.7.key_in, bf16[256,2048]{1,0:T(8,128)(2,1)} %get-tuple-element.8.value_in), custom_call_target="tpu_custom_call" | custom-call | tf_op jit(solution)/shard_map/pallas_call | solution.py:402
